TPU v7x, 32 devices: a whole 2x2x4 slice. The times are simulated.
32 devices in a mesh: grp: 4 (over z), tp: 8 (over y, x, core).
Axes of the slice: x: 2, y: 2, z: 4, core: 2. Of those that a mesh axis runs over, the one named last changes fastest.
Arguments:
- tokens: bfloat16 [2048, 4096], P('grp', 'tp'), may hold values from -6 to 6
- token_tenant: int32 [2048], P('grp'), may hold values from 0 to 63, as said below
- tenant_storage_slot: int32 [64], replicated, may hold values from 0 to 63, as said below
- gate_matrix: bfloat16 [4096, 14336], P(None, 'tp'), may hold values from -0.09375 to 0.09375
- up_matrix: bfloat16 [4096, 14336], P(None, 'tp'), may hold values from -0.09375 to 0.09375
- down_matrix: bfloat16 [14336, 4096], P('tp'), may hold values from -0.046875 to 0.046875
- adapter_gate_up_inputs: bfloat16 [64, 4096, 128], P('grp', 'tp'), may hold values from -0.09375 to 0.09375
- adapter_gate_up_outputs: bfloat16 [64, 128, 14336], P('grp', None, 'tp'), may hold values from -0.75 to 0.75
- adapter_down_inputs: bfloat16 [64, 14336, 64], P('grp', 'tp'), may hold values from -0.046875 to 0.046875
- adapter_down_outputs: bfloat16 [64, 64, 4096], P('grp', None, 'tp'), may hold values from -0.75 to 0.75
Outputs:
- mixed: bfloat16 [2048, 4096], P('grp', 'tp')
Inputs may be any that keep to these rules, and one draw needn't show every extreme that they name: `token_tenant`: within each aligned block of 512 tokens, at most 256 tokens have tenants whose slot lies in one storage block of 16 slots; one storage block, chosen from the seed, receives exactly 256 tokens from every such block. `tenant_storage_slot`: A permutation of the tenants.
All inputs are finite; a program needn't handle non-finite values.
Results may differ from a plain program's by a relative error of at most 0.017.
Values may be sent and summed in bfloat16 or wider, within the bound.
A program may use at most 128 MiB of HBM per device.

v0:
```python
import jax
import jax.numpy as jnp
from jax import lax
from jax.sharding import PartitionSpec as P


def spread_onehot(onehot, vec):
    wide = onehot[:, :, None] * vec[:, None, :]
    return wide.reshape(vec.shape[0], -1)


def body(
    tokens,
    token_tenant,
    tenant_storage_slot,
    gate_matrix,
    up_matrix,
    down_matrix,
    adapter_gate_up_inputs,
    adapter_gate_up_outputs,
    adapter_down_inputs,
    adapter_down_outputs,
):
    groups = lax.axis_size("grp")
    rows = tokens.shape[0]
    block_slots = adapter_gate_up_inputs.shape[0]
    adapter_width = adapter_gate_up_inputs.shape[2] // 2
    hidden_share = gate_matrix.shape[1]
    width_share = tokens.shape[1]
    capacity = 2 * rows // groups
    table = jnp.arange(tenant_storage_slot.shape[0], dtype=jnp.int32)
    match = token_tenant[:, None] == table[None, :]
    slot = jnp.sum(jnp.where(match, tenant_storage_slot[None, :], 0), 1)
    server = slot // block_slots
    local = slot - server * block_slots
    picks = (server[:, None] == jnp.arange(groups, dtype=jnp.int32)[None, :]).astype(jnp.int32)
    place = jnp.sum(picks * (jnp.cumsum(picks, 0) - 1), 1)

    def pack(values, fill):
        buffer = jnp.full((groups, capacity) + values.shape[1:], fill, values.dtype)
        return buffer.at[server, place].set(values)

    sent_rows = pack(tokens, 0)
    sent_local = pack(local.astype(jnp.bfloat16), -1)
    got_rows, got_local = (
        lax.all_to_all(sent_rows, "grp", split_axis=0, concat_axis=0, tiled=True),
        lax.all_to_all(sent_local, "grp", split_axis=0, concat_axis=0, tiled=True),
    )
    rows_flattened = got_rows.reshape(groups * capacity, width_share)
    owner = got_local.reshape(-1).astype(jnp.float32)
    onehot = (owner[:, None] == jnp.arange(block_slots, dtype=jnp.float32)[None, :]).astype(
        jnp.bfloat16
    )
    onehot_wide = onehot.astype(jnp.float32)[:, :, None]
    part = jnp.einsum(
        "ny,eyq->neq", rows_flattened, adapter_gate_up_inputs, preferred_element_type=jnp.float32
    )
    part = jnp.sum(part * onehot_wide, 1)
    ranks = lax.psum(part, "tp").astype(jnp.bfloat16)
    gate_output_factor = adapter_gate_up_outputs[:, :adapter_width, :].reshape(
        block_slots * adapter_width, hidden_share
    )
    up_output_factor = adapter_gate_up_outputs[:, adapter_width:, :].reshape(
        block_slots * adapter_width, hidden_share
    )
    delta_gate = jnp.dot(
        spread_onehot(onehot, ranks[:, :adapter_width]),
        gate_output_factor,
        preferred_element_type=jnp.float32,
    ).astype(jnp.bfloat16)
    delta_up = jnp.dot(
        spread_onehot(onehot, ranks[:, adapter_width:]),
        up_output_factor,
        preferred_element_type=jnp.float32,
    ).astype(jnp.bfloat16)
    back_gate, back_up = (
        lax.all_to_all(
            delta_gate.reshape(groups, capacity, hidden_share),
            "grp",
            split_axis=0,
            concat_axis=0,
            tiled=True,
        ),
        lax.all_to_all(
            delta_up.reshape(groups, capacity, hidden_share),
            "grp",
            split_axis=0,
            concat_axis=0,
            tiled=True,
        ),
    )
    piece = lax.all_gather(tokens, "tp", axis=1, tiled=True)
    base_gate = jnp.dot(piece, gate_matrix, preferred_element_type=jnp.float32)
    base_up = jnp.dot(piece, up_matrix, preferred_element_type=jnp.float32)
    gate = base_gate + back_gate[server, place].astype(jnp.float32)
    up = base_up + back_up[server, place].astype(jnp.float32)
    hidden = (jax.nn.silu(gate) * up).astype(jnp.bfloat16)
    sent_hidden = pack(hidden, 0)
    got_hidden = lax.all_to_all(sent_hidden, "grp", split_axis=0, concat_axis=0, tiled=True)
    hidden_flattened = got_hidden.reshape(groups * capacity, hidden_share)
    down_part = jnp.einsum(
        "us,ysc->uyc", hidden_flattened, adapter_down_inputs, preferred_element_type=jnp.float32
    )
    down_part = jnp.sum(down_part * onehot_wide, 1)
    down_ranks = lax.psum(down_part.astype(jnp.bfloat16), "tp")
    down_output_factor = adapter_down_outputs.reshape(block_slots * adapter_width, width_share)
    delta_down = jnp.dot(
        spread_onehot(onehot, down_ranks), down_output_factor, preferred_element_type=jnp.float32
    ).astype(jnp.bfloat16)
    back_down = lax.all_to_all(
        delta_down.reshape(groups, capacity, width_share),
        "grp",
        split_axis=0,
        concat_axis=0,
        tiled=True,
    )
    returned = back_down[server, place].astype(jnp.float32)
    flipped = lax.psum_scatter(
        lax.dot_general(
            down_matrix, hidden, (((0,), (1,)), ((), ())), preferred_element_type=jnp.float32
        ).astype(jnp.bfloat16),
        "tp",
        scatter_dimension=0,
        tiled=True,
    ).astype(jnp.float32)
    result = flipped.T + returned
    return result.astype(jnp.bfloat16)


def solution(mesh):
    return jax.shard_map(
        body,
        mesh=mesh,
        in_specs=(
            P("grp", "tp"),
            P("grp"),
            P(),
            P(None, "tp"),
            P(None, "tp"),
            P("tp", None),
            P("grp", "tp", None),
            P("grp", None, "tp"),
            P("grp", "tp", None),
            P("grp", None, "tp"),
        ),
        out_specs=P("grp", "tp"),
        check_vma=False,
    )
```

profile of v0, /device:TPU:0, one launch (start us, length us, event | category | flops | bytes accessed | tf_op | source)
XLA Modules:
  0.0 692.8 jit_solution(9002919948820574996)
XLA Ops:
  6.5 0.9 select_reduce_fusion
  7.5 1.2 reduce-window.6
  9.3 24.9 %scatter_fusion = bf16[4,256]{1,0:T(4,128)(2,1)S(1)} fusion(bf16[4,256]{1,0:T(4,128)(2,1)S(1)} %broadcast_in_dim.18, s32[512]{0:T(512)S(1)} %bitcast.75, bf16[512]{0:T(512)(128)(2,1)S(1)} %get-tuple-element.5), kind=kCustom, calls=%fused_computation.3 | custom fusion | bytes 7168 | tf_op jit(solution)/shard_map/scatter | solution.py:41
  36.0 6.3 all-to-all-start
  42.3 1.1 broadcast_in_dim.21
  43.4 67.7 %scatter_fusion.1 = bf16[4,256,512]{2,1,0:T(8,128)(2,1)} fusion(bf16[4,256,512]{2,1,0:T(8,128)(2,1)} %broadcast_in_dim.21, s32[512]{0:T(512)S(1)} %bitcast.76, bf16[512,512]{1,0:T(8,128)(2,1)S(1)} %copy-done.2), kind=kCustom, calls=%fused_computation.4 | custom fusion | bytes 1576960 | tf_op jit(solution)/shard_map/scatter | solution.py:41
  111.0 5.0 all-to-all-start.1
  116.0 25.1 %all-to-all-done.1 = bf16[4,256,512]{2,1,0:T(8,128)(2,1)S(1)} async-done(((bf16[4,256,512]{2,1,0:T(8,128)(2,1)}), bf16[4,256,512]{2,1,0:T(8,128)(2,1)S(1)}, u32[]{:S(2)}, u32[]{:S(2)}) %all-to-all-start.1) | async-done | bytes 1048608 | tf_op jit(solution)/shard_map/all_to_all | solution.py:46
  141.2 3.7 multiply_reduce_fusion
  144.9 31.1 %all-reduce.4 = bf16[1024,128]{1,0:T(8,128)(2,1)S(1)} all-reduce(f32[1024,128]{1,0:T(8,128)} %multiply_reduce_fusion), channel_id=1, replica_groups=mesh['grp'=4,'tp'=8] {'tp'}, use_global_device_ids=true, to_apply=%region_7.8 | all-reduce | flops 131072 | bytes 786432 | tf_op jit(solution)/shard_map/psum | solution.py:59
  176.3 7.5 %bitcast_convert_fusion.1 = bf16[1024,1792]{1,0:T(8,128)(2,1)} fusion(bf16[16,128,1792]{2,1,0:T(8,128)(2,1)} %param.17, bf16[1024,64]{0,1:T(8,128)(2,1)S(1)} %copy.17, bf16[1024,16]{0,1:T(8,128)(2,1)S(1)} %get-tuple-element.11), kind=kOutput, calls=%fused_computation.8 | convolution fusion | flops 3760979968 | bytes 7503872 | tf_op jit(solution)/shard_map/dot_general | solution.py:66
  183.8 4.7 all-to-all-start.2
  189.4 7.5 %bitcast_convert_fusion = bf16[1024,1792]{1,0:T(8,128)(2,1)} fusion(bf16[16,128,1792]{2,1,0:T(8,128)(2,1)} %param.17, bf16[1024,64]{0,1:T(8,128)(2,1)S(1)} %copy.18, bf16[1024,16]{0,1:T(8,128)(2,1)S(1)} %get-tuple-element.11), kind=kOutput, calls=%fused_computation.7 | convolution fusion | flops 3760979968 | bytes 7503872 | tf_op jit(solution)/shard_map/dot_general | solution.py:71
  197.0 71.1 %all-to-all-done.2 = bf16[4,256,1792]{2,1,0:T(8,128)(2,1)} async-done(((bf16[4,256,1792]{2,1,0:T(8,128)(2,1)}), bf16[4,256,1792]{2,1,0:T(8,128)(2,1)}, u32[]{:S(2)}, u32[]{:S(2)}) %all-to-all-start.2) | async-done | bytes 3670048 | tf_op jit(solution)/shard_map/all_to_all | solution.py:77
  268.1 4.8 all-to-all-start.3
  273.1 9.6 %gather_fusion = bf16[512,1792]{1,0:T(8,128)(2,1)S(1)} fusion(bf16[4,256,1792]{2,1,0:T(8,128)(2,1)} %all-to-all-done.2, s32[512]{0:T(512)S(1)} %bitcast.72), kind=kCustom, calls=%fused_computation | custom fusion | bytes 3674112 | tf_op jit(solution)/shard_map/gather | solution.py:95
  282.8 71.6 %all-to-all-done.3 = bf16[4,256,1792]{2,1,0:T(8,128)(2,1)} async-done(((bf16[4,256,1792]{2,1,0:T(8,128)(2,1)}), bf16[4,256,1792]{2,1,0:T(8,128)(2,1)}, u32[]{:S(2)}, u32[]{:S(2)}) %all-to-all-start.3) | async-done | bytes 3670048 | tf_op jit(solution)/shard_map/all_to_all | solution.py:84
  354.4 12.5 %gather_fusion.1 = bf16[512,1792]{1,0:T(8,128)(2,1)} fusion(bf16[4,256,1792]{2,1,0:T(8,128)(2,1)} %all-to-all-done.3, s32[512]{0:T(512)S(1)} %bitcast.73), kind=kCustom, calls=%fused_computation.1 | custom fusion | bytes 3674112 | tf_op jit(solution)/shard_map/gather | solution.py:96
  366.8 11.8 %fusion.29 = f32[512,1792]{1,0:T(8,128)S(1)} fusion(bf16[512,4096]{1,0:T(8,128)(2,1)} %all-gather.2.cloned.1.call-done, bf16[4096,1792]{1,0:T(8,128)(2,1)} %param.13), kind=kOutput, calls=%fused_computation.69 | convolution fusion | flops 7516192768 | bytes 22544384 | tf_op jit(solution)/shard_map/dot_general | solution.py:93
  378.7 13.8 %multiply_convert_fusion = bf16[512,1792]{1,0:T(8,128)(2,1)} fusion(bf16[512,1792]{1,0:T(8,128)(2,1)S(1)} %copy-done.3, f32[512,1792]{1,0:T(8,128)S(1)} %fusion.29, bf16[512,1792]{1,0:T(8,128)(2,1)S(1)} %gather_fusion, bf16[512,4096]{1,0:T(8,128)(2,1)S(1)} %copy-done.5, bf16[4096,1792]{1,0:T(8,128)(2,1)} %param.14), kind=kOutput, calls=%fused_computation.12 | convolution fusion | flops 7525367808 | bytes 28049408 | tf_op jit(solution)/shard_map/dot_general | solution.py:94
  392.5 2.0 broadcast_in_dim.22
  394.7 89.9 %scatter_fusion.2 = bf16[4,256,1792]{2,1,0:T(8,128)(2,1)} fusion(bf16[4,256,1792]{2,1,0:T(8,128)(2,1)} %broadcast_in_dim.22, s32[512]{0:T(512)S(1)} %bitcast.77, bf16[512,1792]{1,0:T(8,128)(2,1)S(1)} %copy-done.4), kind=kCustom, calls=%fused_computation.5 | custom fusion | bytes 5509120 | tf_op jit(solution)/shard_map/scatter | solution.py:41
  484.7 85.4 %all_to_all.34 = bf16[4,256,1792]{2,1,0:T(8,128)(2,1)S(1)} all-to-all(bf16[4,256,1792]{2,1,0:T(8,128)(2,1)} %scatter_fusion.2), channel_id=1, replica_groups=mesh['grp'=4,'tp'=8] {'grp'}, dimensions={0} | all-to-all | bytes 7340032 | tf_op jit(solution)/shard_map/all_to_all | solution.py:99
  570.1 4.0 fusion.30
  574.1 1.2 multiply_reduce_fusion.1
  575.4 12.4 %fusion = bf16[4096,512]{0,1:T(8,128)(2,1)} fusion(bf16[512,1792]{1,0:T(8,128)(2,1)S(1)} %copy-done.4, bf16[1792,4096]{1,0:T(8,128)(2,1)} %param.15), kind=kOutput, calls=%fused_computation.10 | convolution fusion | flops 7518289920 | bytes 20709376 | tf_op jit(solution)/shard_map/dot_general | solution.py:119
  587.8 41.9 %all-reduce.3.cloned.1.call-done = bf16[1024,64]{0,1:T(8,128)(2,1)} async-done(((bf16[1024,64]{0,1:T(8,128)(2,1)}), bf16[1024,64]{0,1:T(8,128)(2,1)}) %all-reduce.3.cloned.1.call-update) | async-done | bytes 131088 | tf_op jit(solution)/shard_map/psum | solution.py:105
  629.6 2.2 bitcast_convert_fusion.2
  631.8 29.5 %all_to_all.35 = bf16[4,256,512]{2,1,0:T(8,128)(2,1)S(1)} all-to-all(bf16[4,256,512]{2,1,0:T(8,128)(2,1)S(1)} %bitcast.83), channel_id=1, replica_groups=mesh['grp'=4,'tp'=8] {'grp'}, dimensions={0} | all-to-all | bytes 2097152 | tf_op jit(solution)/shard_map/all_to_all | solution.py:110
  661.3 6.4 gather_fusion.2
  667.7 16.4 %reduce-scatter.2.cloned.1.call-done = bf16[512,512]{0,1:T(8,128)(2,1)} async-done(((bf16[4096,512]{0,1:T(8,128)(2,1)}), bf16[512,512]{0,1:T(8,128)(2,1)}) %reduce-scatter.2.cloned.1.call-update) | async-done | bytes 524304 | tf_op jit(solution)/shard_map/reduce_scatter | solution.py:118
  684.1 2.1 fusion.9
  (42 shorter events, 4.0 us)
Async XLA Ops:
  6.5 134.6 %copy-start = (bf16[16,512,128]{2,1,0:T(8,128)(2,1)S(1)}, bf16[16,512,128]{2,1,0:T(8,128)(2,1)}, u32[]{:S(2)}) copy-start(bf16[16,512,128]{2,1,0:T(8,128)(2,1)} %param.16) | copy-start | bytes 6291460
  6.5 36.8 %copy-start.2 = (bf16[512,512]{1,0:T(8,128)(2,1)S(1)}, bf16[512,512]{1,0:T(8,128)(2,1)}, u32[]{:S(2)}) copy-start(bf16[512,512]{1,0:T(8,128)(2,1)} %param.10) | copy-start | bytes 1572868
  36.0 75.0 %all-to-all-start = ((bf16[4,2,128]{2,1,0:T(2,128)(2,1)}), bf16[4,2,128]{2,1,0:T(2,128)(2,1)S(1)}, u32[]{:S(2)}, u32[]{:S(2)}) async-start(bf16[4,2,128]{2,1,0:T(2,128)(2,1)} %reshape.219), calls=%async_computation | async-start | bytes 4096 | tf_op jit(solution)/shard_map/all_to_all | solution.py:47
  111.0 30.1 %all-to-all-start.1 = ((bf16[4,256,512]{2,1,0:T(8,128)(2,1)}), bf16[4,256,512]{2,1,0:T(8,128)(2,1)S(1)}, u32[]{:S(2)}, u32[]{:S(2)}) async-start(bf16[4,256,512]{2,1,0:T(8,128)(2,1)} %scatter_fusion.1), calls=%async_computation.1 | async-start | bytes 2097152 | tf_op jit(solution)/shard_map/all_to_all | solution.py:46
  183.8 84.2 %all-to-all-start.2 = ((bf16[4,256,1792]{2,1,0:T(8,128)(2,1)}), bf16[4,256,1792]{2,1,0:T(8,128)(2,1)}, u32[]{:S(2)}, u32[]{:S(2)}) async-start(bf16[4,256,1792]{2,1,0:T(8,128)(2,1)} %bitcast.79), calls=%async_computation.2 | async-start | bytes 7340032 | tf_op jit(solution)/shard_map/all_to_all | solution.py:77
  188.6 178.3 %all-gather.2.cloned.1.call-start = ((), (), s32[]{:S(2)}) async-start(), calls=%async_computation.7 | async-start | bytes 4718592 | tf_op jit(solution)/shard_map/all_gather | solution.py:92
  268.1 86.3 %all-to-all-start.3 = ((bf16[4,256,1792]{2,1,0:T(8,128)(2,1)}), bf16[4,256,1792]{2,1,0:T(8,128)(2,1)}, u32[]{:S(2)}, u32[]{:S(2)}) async-start(bf16[4,256,1792]{2,1,0:T(8,128)(2,1)} %bitcast.80), calls=%async_computation.3 | async-start | bytes 7340032 | tf_op jit(solution)/shard_map/all_to_all | solution.py:84
  272.9 356.7 %all-reduce.3.cloned.1.call-start = ((), (), s32[]{:S(2)}) async-start(), calls=%async_computation.9 | async-start | bytes 262144 | tf_op jit(solution)/shard_map/psum | solution.py:105
  366.8 11.8 %copy-start.3 = (bf16[512,1792]{1,0:T(8,128)(2,1)S(1)}, bf16[512,1792]{1,0:T(8,128)(2,1)}, u32[]{:S(2)}) copy-start(bf16[512,1792]{1,0:T(8,128)(2,1)} %gather_fusion.1) | copy-start | bytes 5505028
  366.8 11.9 %copy-start.5 = (bf16[512,4096]{1,0:T(8,128)(2,1)S(1)}, bf16[512,4096]{1,0:T(8,128)(2,1)}, u32[]{:S(2)}) copy-start(bf16[512,4096]{1,0:T(8,128)(2,1)} %all-gather.2.cloned.1.call-done) | copy-start | bytes 12582916
  392.5 2.2 copy-start.4
  484.7 85.4 %copy-start.6 = (bf16[16,1792,64]{1,2,0:T(8,128)(2,1)S(1)}, bf16[16,1792,64]{1,2,0:T(8,128)(2,1)}, u32[]{:S(2)}) copy-start(bf16[16,1792,64]{1,2,0:T(8,128)(2,1)} %param.18) | copy-start | bytes 11010052
  575.3 108.8 %reduce-scatter.2.cloned.1.call-start = ((), (), s32[]{:S(2)}) async-start(), calls=%async_computation.8 | async-start | bytes 4718592 | tf_op jit(solution)/shard_map/reduce_scatter | solution.py:118
  587.7 41.9 %copy-start.7 = (bf16[16,64,512]{2,1,0:T(8,128)(2,1)S(1)}, bf16[16,64,512]{2,1,0:T(8,128)(2,1)}, u32[]{:S(2)}) copy-start(bf16[16,64,512]{2,1,0:T(8,128)(2,1)} %param.19) | copy-start | bytes 3145732
  631.8 54.4 %copy-start.1 = (bf16[16,512,128]{2,1,0:T(8,128)(2,1)S(1)}, bf16[16,512,128]{2,1,0:T(8,128)(2,1)}, u32[]{:S(2)}) copy-start(bf16[16,512,128]{2,1,0:T(8,128)(2,1)} %param.16) | copy-start | bytes 6291460
Sparse Core Ops, SparseCore 0:
  191.3 36.9 all-gather.1
  575.4 54.1 all-reduce.2
  633.4 50.7 reduce-scatter.1
where the time goes:
time: 699 us; the launch traced here: 693 us
  waiting for transfers between devices  227 us (32%)
  local copies, waits for them, and re-layouts  216 us (31%)
  blocking collectives  146 us (21%)
  matrix products  63 us (9%)
  starting transfers between devices  21.2 us (3%)
  between operations  13.3 us (2%)
    scatter x3, local copies, waits for them, and re-layouts, pack(): return buffer.at[server, place].set(values)  182 us
    all_to_all x1, blocking collectives, body(): lax.all_to_all(sent_hidden, 'grp', split_axis=0, concat_axis=0, tiled=True)  85.4 us
    all_to_all x1, waiting for transfers between devices, body(): lax.all_to_all(delta_up.reshape(groups, capacity, hidden_share), 'grp', s...  71.6 us
    all_to_all x1, waiting for transfers between devices, body(): lax.all_to_all(delta_gate.reshape(groups, capacity, hidden_share), 'grp',...  71.1 us
    psum x1, waiting for transfers between devices, body(): down_ranks = lax.psum(down_part.astype(jnp.bfloat16), 'tp')  41.9 us
    psum x1, blocking collectives, body(): ranks = lax.psum(part, 'tp').astype(jnp.bfloat16)  31.1 us
    all_to_all x1, blocking collectives, body(): lax.all_to_all(delta_down.reshape(groups, capacity, width_share), 'grp',...  29.5 us
    all_to_all x1, waiting for transfers between devices, body(): lax.all_to_all(sent_rows, 'grp', split_axis=0, concat_axis=0, tiled=True)  25.1 us
  transfers between devices with their start and end apart: 7, of which 5 were waited for; matrix products, arithmetic and copies ran while one was open for 17% of the time, Pallas kernels for 0%

commit v1 on v0

v1 whole, which is shorter than its diff:
```python
import jax
import jax.numpy as jnp
from jax import lax
from jax.sharding import PartitionSpec as P

F32 = jnp.float32
BF16 = jnp.bfloat16


def slots_of(tenant, storage_slot):
    table = jnp.arange(storage_slot.shape[0], dtype=jnp.int32)
    match = tenant[..., None] == table
    return jnp.sum(jnp.where(match, storage_slot, 0), -1)


def spread_onehot(onehot, vec):
    wide = onehot[:, :, None] * vec[:, None, :]
    return wide.reshape(vec.shape[0], -1)


def dot(a, b):
    return jnp.dot(a, b, preferred_element_type=F32)


def body(
    tokens,
    token_tenant,
    tenant_storage_slot,
    gate_matrix,
    up_matrix,
    down_matrix,
    adapter_gate_up_inputs,
    adapter_gate_up_outputs,
    adapter_down_inputs,
    adapter_down_outputs,
):
    groups = lax.axis_size("grp")
    me = lax.axis_index("grp")
    rows = tokens.shape[0]
    block_slots = adapter_gate_up_inputs.shape[0]
    rank = adapter_gate_up_inputs.shape[2] // 2
    hidden_share = gate_matrix.shape[1]
    width_share = tokens.shape[1]
    capacity = 2 * rows // groups

    slot = slots_of(token_tenant, tenant_storage_slot)
    server = slot // block_slots
    order = jnp.arange(rows, dtype=jnp.int32)
    upto = (order[:, None] >= order[None, :]).astype(BF16)
    picks = (server[:, None] == jnp.arange(groups, dtype=jnp.int32)[None, :]).astype(BF16)
    count = dot(upto, picks)
    place = jnp.sum(picks.astype(F32) * (count - 1.0), 1).astype(jnp.int32)
    target = server * capacity + place
    seat = jnp.arange(groups * capacity, dtype=jnp.int32)
    pack = (seat[:, None] == target[None, :]).astype(BF16)
    sent = dot(pack, tokens).astype(BF16).reshape(groups, capacity, width_share)
    got = lax.all_to_all(sent, "grp", split_axis=0, concat_axis=0, tiled=True)
    got = got.reshape(groups * capacity, width_share)
    piece = lax.all_gather(got, "tp", axis=1, tiled=True)

    all_tenant = lax.all_gather(token_tenant, "grp", axis=0)
    all_slot = slots_of(all_tenant, tenant_storage_slot)
    here = all_slot // block_slots == me
    local = all_slot - me * block_slots
    all_place = dot(here.astype(BF16), upto.T).astype(jnp.int32) - 1
    all_place = jnp.where(here, all_place, -1)
    seats = (
        jnp.arange(capacity, dtype=jnp.int32)[None, :, None] == all_place[:, None, :]
    ).astype(BF16)
    lanes = (local[:, :, None] == jnp.arange(block_slots, dtype=jnp.int32)).astype(BF16)
    onehot = jnp.einsum("gcr,gre->gce", seats, lanes, preferred_element_type=F32)
    onehot = onehot.astype(BF16).reshape(groups * capacity, block_slots)
    onehot_wide = onehot.astype(F32)[:, :, None]

    part = jnp.einsum("ny,eyq->neq", got, adapter_gate_up_inputs, preferred_element_type=F32)
    part = jnp.sum(part * onehot_wide, 1)
    ranks = lax.psum(part, "tp").astype(BF16)
    gate_factor = adapter_gate_up_outputs[:, :rank, :].reshape(block_slots * rank, hidden_share)
    up_factor = adapter_gate_up_outputs[:, rank:, :].reshape(block_slots * rank, hidden_share)
    delta_gate = dot(spread_onehot(onehot, ranks[:, :rank]), gate_factor).astype(BF16)
    delta_up = dot(spread_onehot(onehot, ranks[:, rank:]), up_factor).astype(BF16)

    gate = dot(piece, gate_matrix) + delta_gate.astype(F32)
    up = dot(piece, up_matrix) + delta_up.astype(F32)
    hidden = (jax.nn.silu(gate) * up).astype(BF16)

    down_part = jnp.einsum("us,ysc->uyc", hidden, adapter_down_inputs, preferred_element_type=F32)
    down_part = jnp.sum(down_part * onehot_wide, 1)
    down_ranks = lax.psum(down_part.astype(BF16), "tp")
    down_factor = adapter_down_outputs.reshape(block_slots * rank, width_share)
    delta_down = dot(spread_onehot(onehot, down_ranks), down_factor).astype(BF16)
    base = lax.psum_scatter(
        dot(hidden, down_matrix).astype(BF16), "tp", scatter_dimension=1, tiled=True
    )
    mixed = (base.astype(F32) + delta_down.astype(F32)).astype(BF16)
    back = lax.all_to_all(
        mixed.reshape(groups, capacity, width_share),
        "grp",
        split_axis=0,
        concat_axis=0,
        tiled=True,
    ).reshape(groups * capacity, width_share)
    unpack = (target[:, None] == seat[None, :]).astype(BF16)
    return dot(unpack, back).astype(BF16)


def solution(mesh):
    return jax.shard_map(
        body,
        mesh=mesh,
        in_specs=(
            P("grp", "tp"),
            P("grp"),
            P(),
            P(None, "tp"),
            P(None, "tp"),
            P("tp", None),
            P("grp", "tp", None),
            P("grp", None, "tp"),
            P("grp", "tp", None),
            P("grp", None, "tp"),
        ),
        out_specs=P("grp", "tp"),
        check_vma=False,
    )
```

time: 699 us -> 330 us (0.47)
  local copies, waits for them, and re-layouts: 216 us -> 0.43 us
  waiting for transfers between devices: 227 us -> 104 us
  blocking collectives: 146 us -> 109 us
  matrix products: 63 us -> 99.9 us
  starting transfers between devices: 21.2 us -> 0.09 us
    scatter x3 -> x0, local copies, waits for them, and re-layouts: 182 us -> none  [pack(): return buffer.at[server, place].set(values)]
    all_to_all x4 -> x0, waiting for transfers between devices: 168 us -> none  [the longest x1 71.6 us: body(): lax.all_to_all(delta_up.reshape(groups, capacity, hidden_share), 'grp', s...]
    reduce_scatter x1, waiting for transfers between devices: 16.4 us -> 74.5 us  [body(): lax.psum_scatter(dot(hidden, down_matrix).astype(BF16), 'tp', scatter_dim...]
    all_to_all x2, blocking collectives: 115 us -> 62.1 us  [the longest x1 31.9 us: body(): got = lax.all_to_all(sent, 'grp', split_axis=0, concat_axis=0, tiled=True)]
    dot_general x7 -> x12, matrix products: 59 us -> 93.9 us  [the longest x10 89.3 us: dot(): return jnp.dot(a, b, preferred_element_type=F32)]
    gather x3 -> x0, local copies, waits for them, and re-layouts: 28.5 us -> none  [the longest x1 12.5 us: body(): up = base_up + back_up[server, place].astype(jnp.float32)]
    all_to_all x4 -> x0, starting transfers between devices: 20.8 us -> none  [the longest x1 6.31 us: body(): lax.all_to_all(sent_local, 'grp', split_axis=0, concat_axis=0, tiled=True)]
    psum x1, waiting for transfers between devices: 41.9 us -> 29.6 us  [body(): down_ranks = lax.psum(down_part.astype(BF16), 'tp')]
  transfers between devices with their start and end apart: 7 -> 3, of which waited for: 5 -> 2; matrix products, arithmetic and copies ran while one was open for 17% -> 13% of each run, Pallas kernels for 0% -> 0%
where the time goes in v1:
time: 330 us
  blocking collectives  109 us (33%)
  waiting for transfers between devices  104 us (32%)
  matrix products  99.9 us (30%)
  between operations  13.2 us (4%)
    dot_general x10, matrix products, dot(): return jnp.dot(a, b, preferred_element_type=F32)  89.3 us
    reduce_scatter x1, waiting for transfers between devices, body(): lax.psum_scatter(dot(hidden, down_matrix).astype(BF16), 'tp', scatter_dim...  74.5 us
    psum x1, blocking collectives, body(): ranks = lax.psum(part, 'tp').astype(BF16)  35.3 us
    all_to_all x1, blocking collectives, body(): got = lax.all_to_all(sent, 'grp', split_axis=0, concat_axis=0, tiled=True)  31.9 us
    all_to_all x1, blocking collectives, body(): lax.all_to_all(mixed.reshape(groups, capacity, width_share), 'grp', split...  30.1 us
    psum x1, waiting for transfers between devices, body(): down_ranks = lax.psum(down_part.astype(BF16), 'tp')  29.6 us
    all_gather x1, blocking collectives, body(): all_tenant = lax.all_gather(token_tenant, 'grp', axis=0)  11.9 us
  transfers between devices with their start and end apart: 3, of which 2 were waited for; matrix products, arithmetic and copies ran while one was open for 13% of the time, Pallas kernels for 0%

profile of v1, /device:TPU:0, one launch (start us, length us, event | category | flops | bytes accessed | tf_op | source)
XLA Modules:
  0.0 329.5 jit_solution(15340144636250243862)
XLA Ops:
  6.5 1.0 select_reduce_fusion.1
  7.5 0.3 fusion.20
  7.8 1.8 fusion.9
  9.6 31.9 %all_to_all.10 = bf16[4,256,512]{2,1,0:T(8,128)(2,1)} all-to-all(bf16[4,256,512]{2,1,0:T(8,128)(2,1)S(1)} %bitcast.43), channel_id=1, replica_groups=mesh['grp'=4,'tp'=8] {'grp'}, dimensions={0} | all-to-all | bytes 2097152 | tf_op jit(solution)/shard_map/all_to_all | solution.py:57
  41.5 0.0 copy-done.3
  41.5 0.0 all-gather.4.cloned.1.call-update
  41.6 0.0 all-reduce.3.cloned.1.call-start
  41.6 11.9 %all-gather.1 = s32[4,1,512]{2,1,0:T(1,128)S(1)} all-gather(s32[1,1,512]{2,1,0:T(1,128)S(1)} %bitcast.49), channel_id=2, replica_groups=mesh['grp'=4,'tp'=8] {'grp'}, dimensions={0}, use_global_device_ids=true | all-gather | bytes 10240 | tf_op jit(solution)/shard_map/all_gather | solution.py:61
  53.5 0.0 copy-done.5
  53.5 0.2 select_reduce_fusion
  53.7 0.2 fusion.18
  53.9 0.5 fusion.16
  54.4 4.1 %multiply_reduce_fusion = f32[1024,128]{1,0:T(8,128)S(1)} fusion(f32[1024,16]{0,1:T(8,128)S(1)} %convert_element_type.84, bf16[1024,512,1]{1,0,2:T(8,128)(2,1)} %bitcast.40, bf16[16,512,128]{2,1,0:T(8,128)(2,1)S(1)} %copy-done), kind=kOutput, calls=%fused_computation | convolution fusion | flops 2151546880 | bytes 3735552 | tf_op jit(solution)/shard_map/ny,eyq->neq/dot_general | solution.py:75
  58.5 35.3 %all-reduce.4 = bf16[1024,128]{1,0:T(8,128)(2,1)S(1)} all-reduce(f32[1024,128]{1,0:T(8,128)S(1)} %multiply_reduce_fusion), channel_id=1, replica_groups=mesh['grp'=4,'tp'=8] {'tp'}, use_global_device_ids=true, to_apply=%region_4.5 | all-reduce | flops 131072 | bytes 786432 | tf_op jit(solution)/shard_map/psum | solution.py:77
  93.8 0.1 fusion.50
  94.0 0.1 copy.18
  94.1 0.1 copy.19
  94.3 7.6 %bitcast_convert_fusion = bf16[1024,1792]{1,0:T(8,128)(2,1)} fusion(bf16[16,128,1792]{2,1,0:T(8,128)(2,1)} %param.17, bf16[1024,64]{0,1:T(8,128)(2,1)S(1)} %copy.19, bf16[1024,16]{0,1:T(8,128)(2,1)S(1)} %bitcast.45), kind=kOutput, calls=%fused_computation.2 | convolution fusion | flops 3760979968 | bytes 7503872 | tf_op jit(solution)/shard_map/dot_general | solution.py:22
  101.8 7.5 %bitcast_convert_fusion.1 = bf16[1024,1792]{1,0:T(8,128)(2,1)} fusion(bf16[16,128,1792]{2,1,0:T(8,128)(2,1)} %param.17, bf16[1024,64]{0,1:T(8,128)(2,1)S(1)} %copy.18, bf16[1024,16]{0,1:T(8,128)(2,1)S(1)} %bitcast.46), kind=kOutput, calls=%fused_computation.3 | convolution fusion | flops 3760979968 | bytes 7503872 | tf_op jit(solution)/shard_map/dot_general | solution.py:22
  109.4 21.8 %fusion.51 = f32[1024,1792]{1,0:T(8,128)} fusion(bf16[1024,4096]{1,0:T(8,128)(2,1)} %all-gather.4.cloned.1.call-done, bf16[4096,1792]{1,0:T(8,128)(2,1)} %param.13), kind=kOutput, calls=%fused_computation.79 | convolution fusion | flops 15032385536 | bytes 30408704 | tf_op jit(solution)/shard_map/dot_general | solution.py:22
  131.2 24.3 %multiply_convert_fusion = bf16[1024,1792]{1,0:T(8,128)(2,1)} fusion(bf16[1024,1792]{1,0:T(8,128)(2,1)} %bitcast_convert_fusion, f32[1024,1792]{1,0:T(8,128)} %fusion.51, bf16[1024,1792]{1,0:T(8,128)(2,1)} %bitcast_convert_fusion.1, bf16[1024,4096]{1,0:T(8,128)(2,1)S(1)} %copy-done.6, bf16[4096,1792]{1,0:T(8,128)(2,1)} %param.14), kind=kOutput, calls=%fused_computation.4 | convolution fusion | flops 15050735616 | bytes 41418752 | tf_op jit(solution)/shard_map/dot_general | solution.py:22
  155.5 6.0 %fusion.52 = f32[1024,1024]{0,1:S(1)} fusion(bf16[1024,1792]{1,0:T(8,128)(2,1)} %multiply_convert_fusion, bf16[1792,1024]{0,1:T(8,128)(2,1)S(1)} %bitcast.50), kind=kOutput, calls=%fused_computation.80 | convolution fusion | flops 3758096384 | bytes 11534336
  161.5 1.2 multiply_reduce_fusion.1
  162.7 0.0 all-reduce.3.cloned.1.call-update
  162.7 0.0 reduce-scatter.2.cloned.1.call-start
  162.8 21.6 %convolution_convert_fusion = bf16[1024,4096]{1,0:T(8,128)(2,1)} fusion(bf16[1024,1792]{1,0:T(8,128)(2,1)} %multiply_convert_fusion, bf16[1792,4096]{1,0:T(8,128)(2,1)} %param.15), kind=kOutput, calls=%fused_computation.1 | convolution fusion | flops 15036579840 | bytes 26738688 | tf_op jit(solution)/shard_map/dot_general | solution.py:22
  184.4 0.0 reduce-scatter.2.cloned.1.call-update
  184.4 29.6 %all-reduce.3.cloned.1.call-done = bf16[1024,64]{0,1:T(8,128)(2,1)} async-done(((bf16[1024,64]{0,1:T(8,128)(2,1)}), bf16[1024,64]{0,1:T(8,128)(2,1)}) %all-reduce.3.cloned.1.call-update) | async-done | bytes 131088 | tf_op jit(solution)/shard_map/psum | solution.py:89
  214.0 74.5 %reduce-scatter.2.cloned.1.call-done = bf16[1024,512]{1,0:T(8,128)(2,1)} async-done(((bf16[1024,4096]{1,0:T(8,128)(2,1)}), bf16[1024,512]{1,0:T(8,128)(2,1)}) %reduce-scatter.2.cloned.1.call-update) | async-done | bytes 1048592 | tf_op jit(solution)/shard_map/reduce_scatter | solution.py:92
  288.5 2.7 add_convert_fusion
  291.3 30.1 %all_to_all.11 = bf16[4,256,512]{2,1,0:T(8,128)(2,1)S(1)} all-to-all(bf16[4,256,512]{2,1,0:T(8,128)(2,1)S(1)} %bitcast.41), channel_id=1, replica_groups=mesh['grp'=4,'tp'=8] {'grp'}, dimensions={0} | all-to-all | bytes 2097152 | tf_op jit(solution)/shard_map/all_to_all | solution.py:96
  321.4 1.6 fusion.12
  (24 shorter events, 0.1 us)
Async XLA Ops:
  6.5 47.9 %copy-start = (bf16[16,512,128]{2,1,0:T(8,128)(2,1)S(1)}, bf16[16,512,128]{2,1,0:T(8,128)(2,1)}, u32[]{:S(2)}) copy-start(bf16[16,512,128]{2,1,0:T(8,128)(2,1)} %param.16) | copy-start | bytes 6291460
  6.5 47.0 %copy-start.5 = (s32[64]{0:T(128)S(1)}, s32[64]{0:T(128)}, u32[]{:S(2)}) copy-start(s32[64]{0:T(128)} %param.12) | copy-start | bytes 772
  6.5 35.1 %copy-start.2 = (s32[512]{0:T(512)S(1)}, s32[512]{0:T(512)}, u32[]{:S(2)}) copy-start(s32[512]{0:T(512)} %param.11) | copy-start | bytes 6148
  6.5 102.8 %all-gather.4.cloned.1.call-start = ((), (), s32[]{:S(2)}) async-start(), calls=%async_computation.3 | async-start | bytes 9437184 | tf_op jit(solution)/shard_map/all_gather | solution.py:59
  7.8 33.7 %copy-start.3 = (s32[512]{0:T(512)}, s32[512]{0:T(512)S(1)}, u32[]{:S(2)}) copy-start(s32[512]{0:T(512)S(1)} %convert_add_fusion) | copy-start | bytes 6148
  41.6 172.4 %all-reduce.3.cloned.1.call-start = ((), (), s32[]{:S(2)}) async-start(), calls=%async_computation.5 | async-start | bytes 262144 | tf_op jit(solution)/shard_map/psum | solution.py:89
  109.4 21.8 %copy-start.6 = (bf16[1024,4096]{1,0:T(8,128)(2,1)S(1)}, bf16[1024,4096]{1,0:T(8,128)(2,1)}, u32[]{:S(2)}) copy-start(bf16[1024,4096]{1,0:T(8,128)(2,1)} %all-gather.4.cloned.1.call-done) | copy-start | bytes 25165828
  131.2 24.3 %copy-start.7 = (bf16[16,1792,64]{1,2,0:T(8,128)(2,1)S(1)}, bf16[16,1792,64]{1,2,0:T(8,128)(2,1)}, u32[]{:S(2)}) copy-start(bf16[16,1792,64]{1,2,0:T(8,128)(2,1)} %param.18) | copy-start | bytes 11010052
  162.7 125.8 %reduce-scatter.2.cloned.1.call-start = ((), (), s32[]{:S(2)}) async-start(), calls=%async_computation.4 | async-start | bytes 9437184 | tf_op jit(solution)/shard_map/reduce_scatter | solution.py:92
  184.4 104.2 %copy-start.8 = (bf16[16,64,512]{2,1,0:T(8,128)(2,1)S(1)}, bf16[16,64,512]{2,1,0:T(8,128)(2,1)}, u32[]{:S(2)}) copy-start(bf16[16,64,512]{2,1,0:T(8,128)(2,1)} %param.19) | copy-start | bytes 3145732
  184.4 137.0 %copy-start.4 = (s32[512]{0:T(512)S(1)}, s32[512]{0:T(512)}, u32[]{:S(2)}) copy-start(s32[512]{0:T(512)} %copy-done.3) | copy-start | bytes 6148
  288.5 34.4 %copy-start.1 = (bf16[16,512,128]{2,1,0:T(8,128)(2,1)S(1)}, bf16[16,512,128]{2,1,0:T(8,128)(2,1)}, u32[]{:S(2)}) copy-start(bf16[16,512,128]{2,1,0:T(8,128)(2,1)} %param.16) | copy-start | bytes 6291460
Sparse Core Ops, SparseCore 0:
  41.7 60.1 all-gather.3
  162.8 51.1 all-reduce.2
  217.9 70.6 reduce-scatter.1
